TPU v7x, 32 devices: a whole 2x2x4 slice. The times are simulated.
32 devices in a mesh: gx: 16 (over z, y, core), gy: 2 (over x).
Axes of the slice: x: 2, y: 2, z: 4, core: 2. Of those that a mesh axis runs over, the one named last changes fastest.
Arguments:
- displacement: float32 [3, 128, 16, 128], P(None, 'gx', 'gy'), may hold values from -0.6 to 0.6
- velocity: float32 [3, 128, 16, 128], P(None, 'gx', 'gy'), may hold values from -0.6 to 0.6
- cuts: int32 [16, 128, 16, 128], P(None, 'gx', 'gy'), may hold values from 0 to 3
- material: int32 [128, 16, 128], P('gx', 'gy'), may hold values from 0 to 7
- micromodulus: float32 [8], replicated, may hold values from 0.2 to 2
- cot_disp: float32 [3, 128, 16, 128], P(None, 'gx', 'gy'), may hold values from -6 to 6
- cot_vel: float32 [3, 128, 16, 128], P(None, 'gx', 'gy'), may hold values from -6 to 6
Outputs:
- grad_disp: float32 [3, 128, 16, 128], P(None, 'gx', 'gy')
- grad_vel: float32 [3, 128, 16, 128], P(None, 'gx', 'gy')
- grad_micro: float32 [8], replicated
All inputs are finite; a program needn't handle non-finite values.
Results may differ from a plain program's by a relative error of at most 0.0001.
Values sent between devices are 32-bit elements; how exact they have to be, the bound alone decides.
A program may use at most 128 MiB of HBM per device.

v0:
```python
import math

import jax
import jax.numpy as jnp
from jax import lax
from jax.experimental import pallas as pl
from jax.experimental.pallas import tpu as pltpu
from jax.sharding import PartitionSpec as P

STEPS = 4
NCLASS = 8
TIME_STEP = 0.2
MESH = pl.DeviceIdType.MESH

BONDS = (
    (0, 0, 1),
    (0, 0, 2),
    (0, 1, 0),
    (0, 1, 1),
    (0, 1, -1),
    (0, 2, 0),
    (1, 1, 0),
    (1, 1, 1),
    (1, 1, -1),
    (1, 0, 0),
    (1, 0, 1),
    (1, 0, -1),
    (1, -1, 0),
    (1, -1, 1),
    (1, -1, -1),
    (2, 0, 0),
)
REF_BONDS = (
    (1, 0, 0),
    (0, 1, 0),
    (0, 0, 1),
    (1, 1, 0),
    (1, -1, 0),
    (1, 0, 1),
    (1, 0, -1),
    (0, 1, 1),
    (0, 1, -1),
    (2, 0, 0),
    (0, 2, 0),
    (0, 0, 2),
    (1, 1, 1),
    (1, -1, 1),
    (1, 1, -1),
    (1, -1, -1),
)
CUT_ROW = tuple(REF_BONDS.index(o) for o in BONDS)
UP_Y = range(2, 9)
DOWN_Y = range(12, 15)
DIRS = ((1, 0), (-1, 0), (0, 1), (0, -1), (1, 1), (1, -1), (-1, 1), (-1, -1))
Y0 = 8


def make_kernel(nx, ny, bx, by, nz):
    assert by == 8 and nz == 128
    nf = 2 * STEPS
    inv_nodes = 1.0 / math.sqrt(nx * bx * ny * by * nz)

    def kernel(
        disp, vel, cuts, material, micro, cot_d, cot_v,
        out_a, out_g, out_m,
        fld, rolled_u, rolled_g, stiff, back, vnow, anow, msum,
        pack_y, land_y, pack_c, land_c,
        kpack_u, kland_u, kpack_d, kland_d, kpack_c, kland_c,
        part_x, part_y, mine,
        ssem, rsem, kssem, krsem, psem, qsem,
    ):
        ix = lax.axis_index("gx")
        iy = lax.axis_index("gy")

        def there(sx, sy):
            ok = None
            for pos, step, count in ((ix, sx, nx), (iy, sy, ny)):
                if step:
                    one = (pos + step >= 0) & (pos + step < count)
                    ok = one if ok is None else ok & one
            return ok

        def who(sx, sy):
            return (ix + sx, iy + sy)

        barrier = pltpu.get_barrier_semaphore()
        for j in range(1, nx):
            pl.semaphore_signal(barrier, inc=1, device_id=(lax.rem(ix + j, nx), iy), device_id_type=MESH)
        for j in range(1, ny):
            pl.semaphore_signal(barrier, inc=1, device_id=(ix, lax.rem(iy + j, ny)), device_id_type=MESH)
        for sx, sy in DIRS:
            if sx and sy:
                @pl.when(there(sx, sy))
                def _():
                    pl.semaphore_signal(barrier, inc=1, device_id=who(sx, sy), device_id_type=MESH)

        def copies(f, d):
            sx, sy = DIRS[d]
            if sy == 0:
                a, b = (bx, 0) if sx > 0 else (2, bx + 2)
                src = fld.at[f, :, pl.ds(a, 2), pl.ds(Y0, 8), :]
                dst = fld.at[f, :, pl.ds(b, 2), pl.ds(Y0, 8), :]
            elif sx == 0:
                e = 0 if sy > 0 else 1
                src, dst = pack_y.at[f, e], land_y.at[f, e]
            else:
                src, dst = pack_c.at[f, d - 4], land_c.at[f, d - 4]
            return pltpu.make_async_remote_copy(
                src_ref=src, dst_ref=dst, send_sem=ssem.at[f, d], recv_sem=rsem.at[f, d],
                device_id=who(sx, sy), device_id_type=MESH,
            )

        def send_field(f):
            for d in (0, 1):
                @pl.when(there(*DIRS[d]))
                def _():
                    copies(f, d).start()
            for d in (4, 5, 6, 7):
                sx, sy = DIRS[d]
                x0 = bx if sx > 0 else 2
                y0 = Y0 + 6 if sy > 0 else Y0
                @pl.when(there(sx, sy))
                def _():
                    for c in range(3):
                        for i in range(2):
                            pack_c[f, d - 4, pl.ds(c * 4 + i * 2, 2), :] = fld[f, c, x0 + i, pl.ds(y0, 2), :]
                    copies(f, d).start()
            for d in (2, 3):
                sx, sy = DIRS[d]
                y0 = Y0 + 6 if sy > 0 else Y0
                @pl.when(there(sx, sy))
                def _():
                    for c in range(3):
                        for i in range(bx):
                            pack_y[f, d - 2, pl.ds((c * bx + i) * 2, 2), :] = fld[f, c, 2 + i, pl.ds(y0, 2), :]
                    copies(f, d).start()

        def recv_field(f):
            for d in range(8):
                sx, sy = DIRS[d]
                y0 = Y0 - 2 if sy > 0 else Y0 + 8
                @pl.when(there(-sx, -sy))
                def _():
                    copies(f, d).wait_recv()
                    for c in range(3):
                        if sx == 0:
                            for i in range(bx):
                                fld[f, c, 2 + i, pl.ds(y0, 2), :] = land_y[f, d - 2, pl.ds((c * bx + i) * 2, 2), :]
                        elif sy:
                            x0 = 0 if sx > 0 else bx + 2
                            for i in range(2):
                                fld[f, c, x0 + i, pl.ds(y0, 2), :] = land_c[f, d - 4, pl.ds(c * 4 + i * 2, 2), :]

        for c in range(3):
            for x in range(bx):
                fld[0, c, 2 + x, pl.ds(Y0, 8), :] = disp[c, x]
                vnow[c, x] = vel[c, x]
                anow[c, x] = cot_d[c, x]
                fld[2 * STEPS - 1, c, 2 + x, pl.ds(Y0, 8), :] = cot_v[c, x] + TIME_STEP * cot_d[c, x]

        zero = jnp.zeros((8, nz), jnp.float32)
        zero24 = jnp.zeros((24, nz), jnp.float32)

        count = nx - 1 + ny - 1
        diag = jnp.int32(0)
        for sx, sy in DIRS:
            if sx and sy:
                diag = diag + jnp.where(there(sx, sy), 1, 0).astype(jnp.int32)
        pl.semaphore_wait(barrier, diag + count)

        send_field(0)

        py = lax.broadcasted_iota(jnp.int32, (8, nz), 0) + iy * by
        pz = lax.broadcasted_iota(jnp.int32, (8, nz), 1)

        def own_stiff(x, carry):
            mat = material[x]
            mu = jnp.zeros((8, nz), jnp.float32)
            for cl in range(NCLASS):
                mu = jnp.where(mat == cl, micro[cl], mu)
            px = jnp.full((8, nz), ix * bx + x, jnp.int32)
            for k, (dx, dy, dz) in enumerate(BONDS):
                ok = None
                for pos, step, total in ((px, dx, nx * bx), (py, dy, ny * by), (pz, dz, nz)):
                    if step:
                        one = pos < total - step if step > 0 else pos >= -step
                        ok = one if ok is None else ok & one
                n2 = dx * dx + dy * dy + dz * dz
                scaled = mu * (0.5 / (n2 * math.sqrt(n2)))
                keep = scaled / (1.0 + cuts[CUT_ROW[k], x].astype(jnp.float32))
                stiff[k, 2 + x, pl.ds(Y0, 8), :] = jnp.where(ok, keep, 0.0)
            return carry

        lax.fori_loop(0, bx, own_stiff, 0)

        def kcopies():
            return (
                (1, 0, stiff.at[pl.ds(6, 9), bx + 1, pl.ds(Y0, 8), :], stiff.at[pl.ds(6, 9), 1, pl.ds(Y0, 8), :]),
                (1, 0, stiff.at[15, pl.ds(bx, 2), pl.ds(Y0, 8), :], stiff.at[15, pl.ds(0, 2), pl.ds(Y0, 8), :]),
                (1, 1, kpack_c.at[0], kland_c.at[0]),
                (1, -1, kpack_c.at[1], kland_c.at[1]),
                (0, -1, kpack_d, kland_d),
                (0, 1, kpack_u, kland_u),
            )

        def kcopy(j):
            sx, sy, src, dst = kcopies()[j]
            return pltpu.make_async_remote_copy(
                src_ref=src, dst_ref=dst, send_sem=kssem.at[j], recv_sem=krsem.at[j],
                device_id=who(sx, sy), device_id_type=MESH,
            )

        KDIRS = ((1, 0), (1, 0), (1, 1), (1, -1), (0, -1), (0, 1))
        for j, (sx, sy) in enumerate(KDIRS):
            @pl.when(there(sx, sy))
            def _():
                row = Y0 + 7 if sy > 0 else Y0
                if j == 2 or j == 3:
                    for n, k in enumerate((6, 7, 8) if j == 2 else (12, 13, 14)):
                        kpack_c[j - 2, pl.ds(n, 1), :] = stiff[k, bx + 1, pl.ds(row, 1), :]
                if j == 4:
                    for n, k in enumerate(DOWN_Y):
                        for x in range(bx):
                            kpack_d[pl.ds(n * bx + x, 1), :] = stiff[k, 2 + x, pl.ds(row, 1), :]
                if j == 5:
                    for n, k in enumerate(UP_Y):
                        for x in range(bx):
                            kpack_u[pl.ds(n * bx + x, 1), :] = stiff[k, 2 + x, pl.ds(row, 1), :]
                    for x in range(bx):
                        kpack_u[pl.ds(7 * bx + x, 1), :] = stiff[5, 2 + x, pl.ds(row - 1, 1), :]
                kcopy(j).start()

        send_field(2 * STEPS - 1)

        for cond, planes in ((ix == 0, (0, 1)), (ix == nx - 1, (bx + 2, bx + 3))):
            @pl.when(cond)
            def _():
                for f in range(nf):
                    for c in range(3):
                        for x in planes:
                            fld[f, c, x] = zero24
                if planes[0] == 0:
                    for k in range(6, 16):
                        for x in planes:
                            stiff[k, x] = zero24
        for cond, row in ((iy == 0, 0), (iy == ny - 1, 16)):
            @pl.when(cond)
            def _():
                def clear(x, carry):
                    for f in range(nf):
                        for c in range(3):
                            fld[f, c, x, pl.ds(row, 8), :] = zero
                    for k in UP_Y if row == 0 else DOWN_Y:
                        stiff[k, x, pl.ds(row, 8), :] = zero
                    return carry
                lax.fori_loop(0, bx + 4, clear, 0)

        recv_field(0)

        for j, (sx, sy) in enumerate(KDIRS):
            @pl.when(there(-sx, -sy))
            def _():
                kcopy(j).wait_recv()
                row = Y0 - 1 if sy > 0 else Y0 + 8
                if j == 2 or j == 3:
                    for n, k in enumerate((6, 7, 8) if j == 2 else (12, 13, 14)):
                        stiff[k, 1, pl.ds(row, 1), :] = kland_c[j - 2, pl.ds(n, 1), :]
                if j == 4:
                    for n, k in enumerate(DOWN_Y):
                        for x in range(bx):
                            stiff[k, 2 + x, pl.ds(row, 1), :] = kland_d[pl.ds(n * bx + x, 1), :]
                if j == 5:
                    for n, k in enumerate(UP_Y):
                        for x in range(bx):
                            stiff[k, 2 + x, pl.ds(row, 1), :] = kland_u[pl.ds(n * bx + x, 1), :]
                    for x in range(bx):
                        stiff[5, 2 + x, pl.ds(row - 1, 1), :] = kland_u[pl.ds(7 * bx + x, 1), :]

        def back_stiff(x, carry):
            for k, (dx, dy, dz) in enumerate(BONDS):
                val = stiff[k, 2 + x - dx, pl.ds(Y0 - dy, 8), :]
                if dz:
                    val = pltpu.roll(val, dz % nz, 1)
                back[k, x] = val
            return carry

        lax.fori_loop(0, bx, back_stiff, 0)

        def roll_field(f, out):
            def one(x, carry):
                for c in range(3):
                    for r in (Y0 - 1, Y0 + 1):
                        val = fld[f, c, x, pl.ds(r, 8), :]
                        out[0, c, x, pl.ds(r, 8), :] = pltpu.roll(val, nz - 1, 1)
                        out[1, c, x, pl.ds(r, 8), :] = pltpu.roll(val, 1, 1)
                return carry
            lax.fori_loop(1, bx + 3, one, 0)

        def get(f, out, c, x, off, centre):
            dx, dy, dz = off
            if abs(dz) == 2:
                return pltpu.roll(centre, (-dz) % nz, 1)
            if dz:
                return out[0 if dz > 0 else 1, c, x + 2 + dx, pl.ds(Y0 + dy, 8), :]
            return fld[f, c, x + 2 + dx, pl.ds(Y0 + dy, 8), :]

        def bond_list():
            for k, o in enumerate(BONDS):
                yield k, False, o
                yield k, True, tuple(-e for e in o)

        def coef(k, rev, x):
            return back[k, x] if rev else stiff[k, x + 2, pl.ds(Y0, 8), :]

        def vectors(f, x, off, cent, shifted):
            return [get(f, rolled_u, c, x, off, cent[c]) - shifted[c][off[c]] for c in range(3)]

        def centres(f, x):
            cent = [fld[f, c, x + 2, pl.ds(Y0, 8), :] for c in range(3)]
            shifted = [{e: cent[c] - float(e) for e in (-2, -1, 0, 1, 2)} for c in range(3)]
            return cent, shifted

        def forward(n):
            roll_field(n, rolled_u)

            def one(x, carry):
                cent, shifted = centres(n, x)
                acc = [jnp.zeros((8, nz), jnp.float32)] * 3
                for k, rev, off in bond_list():
                    w = vectors(n, x, off, cent, shifted)
                    n2 = float(sum(e * e for e in off))
                    s = (w[0] * w[0] + w[1] * w[1] + w[2] * w[2]) - n2
                    t = coef(k, rev, x) * s
                    acc = [acc[c] + t * w[c] for c in range(3)]
                for c in range(3):
                    v = vnow[c, x] + TIME_STEP * acc[c]
                    vnow[c, x] = v
                    fld[n + 1, c, x + 2, pl.ds(Y0, 8), :] = cent[c] + TIME_STEP * v
                return carry

            lax.fori_loop(0, bx, one, 0)

        def adjoint(n):
            gf = STEPS + n
            roll_field(gf, rolled_g)
            roll_field(n, rolled_u)

            def one(x, carry):
                cent, shifted = centres(n, x)
                gc = [fld[gf, c, x + 2, pl.ds(Y0, 8), :] for c in range(3)]
                acc = [jnp.zeros((8, nz), jnp.float32)] * 3
                bcc = [jnp.zeros((8, nz), jnp.float32)] * 3
                m = jnp.zeros((8, nz), jnp.float32)
                for k, rev, off in bond_list():
                    w = vectors(n, x, off, cent, shifted)
                    g = [gc[c] - get(gf, rolled_g, c, x, off, gc[c]) for c in range(3)]
                    n2 = float(sum(e * e for e in off))
                    s = (w[0] * w[0] + w[1] * w[1] + w[2] * w[2]) - n2
                    dot = w[0] * g[0] + w[1] * g[1] + w[2] * g[2]
                    kk = coef(k, rev, x)
                    t = kk * s
                    r = kk * dot
                    if not rev:
                        m = m + s * r
                    acc = [acc[c] + t * g[c] for c in range(3)]
                    bcc = [bcc[c] + r * w[c] for c in range(3)]
                for c in range(3):
                    a = anow[c, x] - TIME_STEP * (acc[c] + 2.0 * bcc[c])
                    if n:
                        anow[c, x] = a
                        fld[gf - 1, c, x + 2, pl.ds(Y0, 8), :] = gc[c] + TIME_STEP * a
                    else:
                        out_a[c, x] = a
                        out_g[c, x] = gc[c]
                msum[x] = m if n == STEPS - 1 else msum[x] + m
                return carry

            lax.fori_loop(0, bx, one, 0)

        for n in range(STEPS - 1):
            forward(n)
            send_field(n + 1)
            recv_field(n + 1)
        recv_field(2 * STEPS - 1)
        for n in reversed(range(STEPS)):
            adjoint(n)
            if n:
                send_field(STEPS + n - 1)
                recv_field(STEPS + n - 1)

        lane = lax.broadcasted_iota(jnp.int32, (1, nz), 1)
        row = jnp.zeros((1, nz), jnp.float32)
        for cl in range(NCLASS):
            tot = jnp.zeros((8, nz), jnp.float32)
            for x in range(bx):
                tot = tot + jnp.where(material[x] == cl, msum[x], 0.0)
            one = jnp.sum(jnp.sum(tot, axis=0, keepdims=True), axis=1, keepdims=True)
            row = jnp.where(lane == cl, one * (TIME_STEP * inv_nodes) / micro[cl], row)
        mine[0] = row

        def spread(src, land, axis_pos, size, ident, sems):
            outs = []
            for j in range(1, size):
                cp = pltpu.make_async_remote_copy(
                    src_ref=src, dst_ref=land.at[j - 1], send_sem=sems.at[0, j - 1], recv_sem=sems.at[1, j - 1],
                    device_id=ident(lax.rem(axis_pos + j, size)), device_id_type=MESH,
                )
                cp.start()
                outs.append(cp)
            return outs

        outs = spread(mine.at[0], part_x, ix, nx, lambda j: (j, iy), psem)
        for cp in outs:
            cp.wait_recv()
        tot = mine[0]
        for j in range(nx - 1):
            tot = tot + part_x[j]
        mine[1] = tot
        outs_y = spread(mine.at[1], part_y, iy, ny, lambda j: (ix, j), qsem)
        for cp in outs_y:
            cp.wait_recv()
        for j in range(ny - 1):
            tot = tot + part_y[j]
        out_m[...] = tot

        for cp in outs + outs_y:
            cp.wait_send()
        for f in range(nf):
            for d in range(8):
                @pl.when(there(*DIRS[d]))
                def _():
                    copies(f, d).wait_send()
        for j, (sx, sy) in enumerate(KDIRS):
            @pl.when(there(sx, sy))
            def _():
                kcopy(j).wait_send()

    return kernel


def solution(mesh):
    nx, ny = mesh.shape["gx"], mesh.shape["gy"]

    def body(displacement, velocity, cuts, material, micromodulus, cot_disp, cot_vel):
        bx, by, nz = material.shape
        nf = 2 * STEPS
        f32 = jnp.float32
        vmem = pl.BlockSpec(memory_space=pltpu.VMEM)
        smem = pl.BlockSpec(memory_space=pltpu.SMEM)
        grad_a, grad_g, micro = pl.pallas_call(
            make_kernel(nx, ny, bx, by, nz),
            out_shape=(
                jax.ShapeDtypeStruct((3, bx, by, nz), f32),
                jax.ShapeDtypeStruct((3, bx, by, nz), f32),
                jax.ShapeDtypeStruct((1, nz), f32),
            ),
            in_specs=[vmem] * 4 + [smem] + [vmem] * 2,
            out_specs=(vmem, vmem, vmem),
            scratch_shapes=[
                pltpu.VMEM((nf, 3, bx + 4, 24, nz), f32),
                pltpu.VMEM((2, 3, bx + 4, 24, nz), f32),
                pltpu.VMEM((2, 3, bx + 4, 24, nz), f32),
                pltpu.VMEM((16, bx + 4, 24, nz), f32),
                pltpu.VMEM((16, bx, 8, nz), f32),
                pltpu.VMEM((3, bx, 8, nz), f32),
                pltpu.VMEM((3, bx, 8, nz), f32),
                pltpu.VMEM((bx, 8, nz), f32),
                pltpu.VMEM((nf, 2, 6 * bx, nz), f32),
                pltpu.VMEM((nf, 2, 6 * bx, nz), f32),
                pltpu.VMEM((nf, 4, 16, nz), f32),
                pltpu.VMEM((nf, 4, 16, nz), f32),
                pltpu.VMEM((8 * bx, nz), f32),
                pltpu.VMEM((8 * bx, nz), f32),
                pltpu.VMEM((3 * bx, nz), f32),
                pltpu.VMEM((3 * bx, nz), f32),
                pltpu.VMEM((2, 8, nz), f32),
                pltpu.VMEM((2, 8, nz), f32),
                pltpu.VMEM((nx, 1, nz), f32),
                pltpu.VMEM((ny, 1, nz), f32),
                pltpu.VMEM((2, 1, nz), f32),
                pltpu.SemaphoreType.DMA((nf, 8)),
                pltpu.SemaphoreType.DMA((nf, 8)),
                pltpu.SemaphoreType.DMA((6,)),
                pltpu.SemaphoreType.DMA((6,)),
                pltpu.SemaphoreType.DMA((2, nx)),
                pltpu.SemaphoreType.DMA((2, ny)),
            ],
            compiler_params=pltpu.CompilerParams(
                collective_id=0, has_side_effects=True, vmem_limit_bytes=40 * 1024 * 1024
            ),
        )(displacement, velocity, cuts, material, micromodulus, cot_disp, cot_vel)
        return grad_a, grad_g, micro[0, :NCLASS]

    return jax.shard_map(
        body,
        mesh=mesh,
        in_specs=(
            P(None, "gx", "gy", None),
            P(None, "gx", "gy", None),
            P(None, "gx", "gy", None),
            P("gx", "gy", None),
            P(),
            P(None, "gx", "gy", None),
            P(None, "gx", "gy", None),
        ),
        out_specs=(P(None, "gx", "gy", None), P(None, "gx", "gy", None), P()),
        check_vma=False,
    )
```

profile of v0, /device:TPU:0, one launch (start us, length us, event | category | flops | bytes accessed | tf_op | source)
XLA Modules:
  0.0 65.1 jit_solution(11085763419881434044)
XLA Ops:
  0.6 0.0 copy-start
  0.6 1.0 %copy-done = s32[16,8,8,128]{3,2,1,0:T(8,128)S(1)} copy-done((s32[16,8,8,128]{3,2,1,0:T(8,128)S(1)}, s32[16,8,8,128]{3,2,1,0:T(8,128)}, u32[]{:S(2)}) %copy-start) | copy-done | bytes 524312
  1.7 0.0 copy-start.1
  1.7 0.9 %copy-done.1 = f32[3,8,8,128]{3,2,1,0:T(8,128)S(1)} copy-done((f32[3,8,8,128]{3,2,1,0:T(8,128)S(1)}, f32[3,8,8,128]{3,2,1,0:T(8,128)}, u32[]{:S(2)}) %copy-start.1) | copy-done | bytes 98328
  2.6 0.0 copy-start.2
  2.6 0.9 %copy-done.2 = f32[3,8,8,128]{3,2,1,0:T(8,128)S(1)} copy-done((f32[3,8,8,128]{3,2,1,0:T(8,128)S(1)}, f32[3,8,8,128]{3,2,1,0:T(8,128)}, u32[]{:S(2)}) %copy-start.2) | copy-done | bytes 98328
  3.5 0.0 copy-start.3
  3.5 0.9 %copy-done.3 = f32[3,8,8,128]{3,2,1,0:T(8,128)S(1)} copy-done((f32[3,8,8,128]{3,2,1,0:T(8,128)S(1)}, f32[3,8,8,128]{3,2,1,0:T(8,128)}, u32[]{:S(2)}) %copy-start.3) | copy-done | bytes 98328
  4.4 0.0 copy-start.4
  4.4 0.9 %copy-done.4 = f32[3,8,8,128]{3,2,1,0:T(8,128)S(1)} copy-done((f32[3,8,8,128]{3,2,1,0:T(8,128)S(1)}, f32[3,8,8,128]{3,2,1,0:T(8,128)}, u32[]{:S(2)}) %copy-start.4) | copy-done | bytes 98328
  5.2 0.0 copy-start.5
  5.2 0.8 %copy-done.5 = s32[8,8,128]{2,1,0:T(8,128)S(1)} copy-done((s32[8,8,128]{2,1,0:T(8,128)S(1)}, s32[8,8,128]{2,1,0:T(8,128)}, u32[]{:S(2)}) %copy-start.5) | copy-done | bytes 32792
  6.0 0.0 copy-start.6
  6.0 0.7 %copy-done.6 = f32[8]{0:T(128)S(1)} copy-done((f32[8]{0:T(128)S(1)}, f32[8]{0:T(128)}, u32[]{:S(2)}) %copy-start.6) | copy-done | bytes 56
  6.7 56.7 %shard_map.94 = (f32[3,8,8,128]{3,2,1,0:T(8,128)S(1)}, f32[3,8,8,128]{3,2,1,0:T(8,128)S(1)}, f32[1,128]{1,0:T(1,128)S(1)}) custom-call(f32[3,8,8,128]{3,2,1,0:T(8,128)S(1)} %copy-done.1, f32[3,8,8,128]{3,2,1,0:T(8,128)S(1)} %copy-done.2, s32[16,8,8,128]{3,2,1,0:T(8,128)S(1)} %copy-done, s32[8,8,128]{2,1,0:T(8,128)S(1)} %copy-done.5, f32[8]{0:T(128)S(1)} %copy-done.6, ...), custom_call_target="tpu_custom_call" | custom-call | tf_op jit(solution)/shard_map/pallas_call | solution.py:450
  63.3 0.5 slice_bitcast_fusion
  63.9 0.6 copy.12
  64.5 0.6 copy.13
Async XLA Ops:
  0.6 1.0 %copy-start = (s32[16,8,8,128]{3,2,1,0:T(8,128)S(1)}, s32[16,8,8,128]{3,2,1,0:T(8,128)}, u32[]{:S(2)}) copy-start(s32[16,8,8,128]{3,2,1,0:T(8,128)} %cuts.1) | copy-start | bytes 1572868
  1.7 0.9 %copy-start.1 = (f32[3,8,8,128]{3,2,1,0:T(8,128)S(1)}, f32[3,8,8,128]{3,2,1,0:T(8,128)}, u32[]{:S(2)}) copy-start(f32[3,8,8,128]{3,2,1,0:T(8,128)} %disp.1) | copy-start | bytes 294916
  2.6 0.9 %copy-start.2 = (f32[3,8,8,128]{3,2,1,0:T(8,128)S(1)}, f32[3,8,8,128]{3,2,1,0:T(8,128)}, u32[]{:S(2)}) copy-start(f32[3,8,8,128]{3,2,1,0:T(8,128)} %vel.1) | copy-start | bytes 294916
  3.5 0.9 %copy-start.3 = (f32[3,8,8,128]{3,2,1,0:T(8,128)S(1)}, f32[3,8,8,128]{3,2,1,0:T(8,128)}, u32[]{:S(2)}) copy-start(f32[3,8,8,128]{3,2,1,0:T(8,128)} %cot_d.1) | copy-start | bytes 294916
  4.4 0.9 %copy-start.4 = (f32[3,8,8,128]{3,2,1,0:T(8,128)S(1)}, f32[3,8,8,128]{3,2,1,0:T(8,128)}, u32[]{:S(2)}) copy-start(f32[3,8,8,128]{3,2,1,0:T(8,128)} %cot_v.1) | copy-start | bytes 294916
  5.2 0.8 %copy-start.5 = (s32[8,8,128]{2,1,0:T(8,128)S(1)}, s32[8,8,128]{2,1,0:T(8,128)}, u32[]{:S(2)}) copy-start(s32[8,8,128]{2,1,0:T(8,128)} %material.1) | copy-start | bytes 98308
  6.0 0.7 %copy-start.6 = (f32[8]{0:T(128)S(1)}, f32[8]{0:T(128)}, u32[]{:S(2)}) copy-start(f32[8]{0:T(128)} %micro.1) | copy-start | bytes 100
where the time goes:
time: 65.5 us; the launch traced here: 65.1 us
  Pallas kernels  56.7 us (87%)
  local copies, waits for them, and re-layouts  7.81 us (12%)
  between operations  0.66 us (1%)
    pallas_call x1, Pallas kernels, body(): pl.pallas_call(make_kernel(nx, ny, bx, by, nz), out_shape=(jax.ShapeDtype...  56.7 us
    unnamed x16, local copies, waits for them, and re-layouts  7.3 us

commit v1 on v0

--- a/solution.py
+++ b/solution.py
@@ -61,13 +61,13 @@
     inv_nodes = 1.0 / math.sqrt(nx * bx * ny * by * nz)
 
     def kernel(
-        disp, vel, cuts, material, micro, cot_d, cot_v,
+        disp, vel, cuts_in, material_in, micro, cot_d, cot_v,
         out_a, out_g, out_m,
-        fld, rolled_u, rolled_g, stiff, back, vnow, anow, msum,
-        pack_y, land_y, pack_c, land_c,
+        fld, rolled, cuts, material, cot_in, tval, stiff, back, vnow, anow, msum,
+        pack_y, land_y, roll_y, pack_c, land_c,
         kpack_u, kland_u, kpack_d, kland_d, kpack_c, kland_c,
-        part_x, part_y, mine,
-        ssem, rsem, kssem, krsem, psem, qsem,
+        part, mine,
+        isem, ssem, rsem, kssem, krsem, psem, qsem,
     ):
         ix = lax.axis_index("gx")
         iy = lax.axis_index("gy")
@@ -84,15 +84,31 @@
             return (ix + sx, iy + sy)
 
         barrier = pltpu.get_barrier_semaphore()
-        for j in range(1, nx):
-            pl.semaphore_signal(barrier, inc=1, device_id=(lax.rem(ix + j, nx), iy), device_id_type=MESH)
-        for j in range(1, ny):
-            pl.semaphore_signal(barrier, inc=1, device_id=(ix, lax.rem(iy + j, ny)), device_id_type=MESH)
-        for sx, sy in DIRS:
-            if sx and sy:
-                @pl.when(there(sx, sy))
-                def _():
-                    pl.semaphore_signal(barrier, inc=1, device_id=who(sx, sy), device_id_type=MESH)
+        me = ix * ny + iy
+
+        def peer(j):
+            to = lax.rem(me + j, nx * ny)
+            return (to // ny, lax.rem(to, ny))
+
+        def greet(j, carry):
+            pl.semaphore_signal(barrier, inc=1, device_id=peer(j), device_id_type=MESH)
+            return carry
+
+        lax.fori_loop(1, nx * ny, greet, 0)
+
+        loads = [
+            pltpu.make_async_copy(src, dst, isem.at[j])
+            for j, (src, dst) in enumerate((
+                (cuts_in, cuts),
+                (material_in, material),
+                (disp, fld.at[0, :, pl.ds(2, bx), pl.ds(Y0, 8), :]),
+                (cot_v, cot_in),
+                (cot_d, anow),
+                (vel, vnow),
+            ))
+        ]
+        for cp in loads:
+            cp.start()
 
         def copies(f, d):
             sx, sy = DIRS[d]
@@ -135,40 +151,60 @@
                             pack_y[f, d - 2, pl.ds((c * bx + i) * 2, 2), :] = fld[f, c, 2 + i, pl.ds(y0, 2), :]
                     copies(f, d).start()
 
+        def turn(val, dz):
+            return pltpu.roll(val, (-dz) % nz, 1)
+
+        def roll_own(f):
+            def some(i, carry):
+                for c in range(3):
+                    for x in range(4):
+                        val = fld[f, c, 2 + i * 4 + x, pl.ds(Y0, 8), :]
+                        rolled[f, 0, c, 2 + i * 4 + x, pl.ds(Y0, 8), :] = turn(val, 1)
+                        rolled[f, 1, c, 2 + i * 4 + x, pl.ds(Y0, 8), :] = turn(val, -1)
+                return carry
+            lax.fori_loop(0, bx // 4, some, 0)
+
         def recv_field(f):
             for d in range(8):
                 sx, sy = DIRS[d]
                 y0 = Y0 - 2 if sy > 0 else Y0 + 8
+                near = Y0 - 1 if sy > 0 else Y0 + 8
+                j0 = 1 if sy > 0 else 0
                 @pl.when(there(-sx, -sy))
                 def _():
                     copies(f, d).wait_recv()
-                    for c in range(3):
-                        if sx == 0:
+                    if sy == 0:
+                        x = 1 if sx > 0 else bx + 2
+                        for c in range(3):
+                            val = fld[f, c, x, pl.ds(Y0, 8), :]
+                            rolled[f, 0, c, x, pl.ds(Y0, 8), :] = turn(val, 1)
+                            rolled[f, 1, c, x, pl.ds(Y0, 8), :] = turn(val, -1)
+                    elif sx == 0:
+                        for i in range(6 * bx // 8):
+                            val = land_y[f, d - 2, pl.ds(i * 8, 8), :]
+                            roll_y[0, pl.ds(i * 8, 8), :] = turn(val, 1)
+                            roll_y[1, pl.ds(i * 8, 8), :] = turn(val, -1)
+                        for c in range(3):
                             for i in range(bx):
-                                fld[f, c, 2 + i, pl.ds(y0, 2), :] = land_y[f, d - 2, pl.ds((c * bx + i) * 2, 2), :]
-                        elif sy:
-                            x0 = 0 if sx > 0 else bx + 2
-                            for i in range(2):
-                                fld[f, c, x0 + i, pl.ds(y0, 2), :] = land_c[f, d - 4, pl.ds(c * 4 + i * 2, 2), :]
-
-        for c in range(3):
-            for x in range(bx):
-                fld[0, c, 2 + x, pl.ds(Y0, 8), :] = disp[c, x]
-                vnow[c, x] = vel[c, x]
-                anow[c, x] = cot_d[c, x]
-                fld[2 * STEPS - 1, c, 2 + x, pl.ds(Y0, 8), :] = cot_v[c, x] + TIME_STEP * cot_d[c, x]
+                                r = (c * bx + i) * 2
+                                fld[f, c, 2 + i, pl.ds(y0, 2), :] = land_y[f, d - 2, pl.ds(r, 2), :]
+                                for z in range(2):
+                                    rolled[f, z, c, 2 + i, pl.ds(near, 1), :] = roll_y[z, pl.ds(r + j0, 1), :]
+                    else:
+                        x = 1 if sx > 0 else bx + 2
+                        i = 1 if sx > 0 else 0
+                        for h in range(2):
+                            val = land_c[f, d - 4, pl.ds(h * 8, 8), :]
+                            roll_y[0, pl.ds(h * 8, 8), :] = turn(val, 1)
+                            roll_y[1, pl.ds(h * 8, 8), :] = turn(val, -1)
+                        for c in range(3):
+                            r = c * 4 + i * 2 + j0
+                            fld[f, c, x, pl.ds(near, 1), :] = land_c[f, d - 4, pl.ds(r, 1), :]
+                            for z in range(2):
+                                rolled[f, z, c, x, pl.ds(near, 1), :] = roll_y[z, pl.ds(r, 1), :]
 
         zero = jnp.zeros((8, nz), jnp.float32)
         zero24 = jnp.zeros((24, nz), jnp.float32)
-
-        count = nx - 1 + ny - 1
-        diag = jnp.int32(0)
-        for sx, sy in DIRS:
-            if sx and sy:
-                diag = diag + jnp.where(there(sx, sy), 1, 0).astype(jnp.int32)
-        pl.semaphore_wait(barrier, diag + count)
-
-        send_field(0)
 
         py = lax.broadcasted_iota(jnp.int32, (8, nz), 0) + iy * by
         pz = lax.broadcasted_iota(jnp.int32, (8, nz), 1)
@@ -191,7 +227,18 @@
                 stiff[k, 2 + x, pl.ds(Y0, 8), :] = jnp.where(ok, keep, 0.0)
             return carry
 
+        loads[0].wait()
+        loads[1].wait()
         lax.fori_loop(0, bx, own_stiff, 0)
+
+        for cp in loads[2:]:
+            cp.wait()
+        for c in range(3):
+            for x in range(bx):
+                fld[2 * STEPS - 1, c, 2 + x, pl.ds(Y0, 8), :] = cot_in[c, x] + TIME_STEP * anow[c, x]
+
+        pl.semaphore_wait(barrier, nx * ny - 1)
+        send_field(0)
 
         def kcopies():
             return (
@@ -231,6 +278,8 @@
                 kcopy(j).start()
 
         send_field(2 * STEPS - 1)
+        roll_own(0)
+        roll_own(2 * STEPS - 1)
 
         for cond, planes in ((ix == 0, (0, 1)), (ix == nx - 1, (bx + 2, bx + 3))):
             @pl.when(cond)
@@ -239,6 +288,8 @@
                     for c in range(3):
                         for x in planes:
                             fld[f, c, x] = zero24
+                        rolled[f, 0, c, planes[0] if planes[0] else 1] = zero24
+                        rolled[f, 1, c, planes[0] if planes[0] else 1] = zero24
                 if planes[0] == 0:
                     for k in range(6, 16):
                         for x in planes:
@@ -250,6 +301,8 @@
                     for f in range(nf):
                         for c in range(3):
                             fld[f, c, x, pl.ds(row, 8), :] = zero
+                            rolled[f, 0, c, x, pl.ds(row, 8), :] = zero
+                            rolled[f, 1, c, x, pl.ds(row, 8), :] = zero
                     for k in UP_Y if row == 0 else DOWN_Y:
                         stiff[k, x, pl.ds(row, 8), :] = zero
                     return carry
@@ -286,22 +339,12 @@
 
         lax.fori_loop(0, bx, back_stiff, 0)
 
-        def roll_field(f, out):
-            def one(x, carry):
-                for c in range(3):
-                    for r in (Y0 - 1, Y0 + 1):
-                        val = fld[f, c, x, pl.ds(r, 8), :]
-                        out[0, c, x, pl.ds(r, 8), :] = pltpu.roll(val, nz - 1, 1)
-                        out[1, c, x, pl.ds(r, 8), :] = pltpu.roll(val, 1, 1)
-                return carry
-            lax.fori_loop(1, bx + 3, one, 0)
-
-        def get(f, out, c, x, off, centre):
+        def get(f, c, x, off, centre):
             dx, dy, dz = off
             if abs(dz) == 2:
-                return pltpu.roll(centre, (-dz) % nz, 1)
+                return turn(centre, dz)
             if dz:
-                return out[0 if dz > 0 else 1, c, x + 2 + dx, pl.ds(Y0 + dy, 8), :]
+                return rolled[f, 0 if dz > 0 else 1, c, x + 2 + dx, pl.ds(Y0 + dy, 8), :]
             return fld[f, c, x + 2 + dx, pl.ds(Y0 + dy, 8), :]
 
         def bond_list():
@@ -313,24 +356,24 @@
             return back[k, x] if rev else stiff[k, x + 2, pl.ds(Y0, 8), :]
 
         def vectors(f, x, off, cent, shifted):
-            return [get(f, rolled_u, c, x, off, cent[c]) - shifted[c][off[c]] for c in range(3)]
+            return [get(f, c, x, off, cent[c]) - shifted[c][off[c]] for c in range(3)]
 
         def centres(f, x):
             cent = [fld[f, c, x + 2, pl.ds(Y0, 8), :] for c in range(3)]
             shifted = [{e: cent[c] - float(e) for e in (-2, -1, 0, 1, 2)} for c in range(3)]
             return cent, shifted
 
+        def stretch(w, off):
+            return (w[0] * w[0] + w[1] * w[1] + w[2] * w[2]) - float(sum(e * e for e in off))
+
         def forward(n):
-            roll_field(n, rolled_u)
-
             def one(x, carry):
                 cent, shifted = centres(n, x)
                 acc = [jnp.zeros((8, nz), jnp.float32)] * 3
                 for k, rev, off in bond_list():
                     w = vectors(n, x, off, cent, shifted)
-                    n2 = float(sum(e * e for e in off))
-                    s = (w[0] * w[0] + w[1] * w[1] + w[2] * w[2]) - n2
-                    t = coef(k, rev, x) * s
+                    t = coef(k, rev, x) * stretch(w, off)
+                    tval[n, 2 * k + rev, x] = t
                     acc = [acc[c] + t * w[c] for c in range(3)]
                 for c in range(3):
                     v = vnow[c, x] + TIME_STEP * acc[c]
@@ -340,10 +383,24 @@
 
             lax.fori_loop(0, bx, one, 0)
 
+        def micro_part():
+            def one(x, carry):
+                cent, shifted = centres(0, x)
+                gc = [fld[STEPS, c, x + 2, pl.ds(Y0, 8), :] for c in range(3)]
+                m = msum[x]
+                for k, rev, off in bond_list():
+                    if rev:
+                        continue
+                    w = vectors(0, x, off, cent, shifted)
+                    g = [gc[c] - get(STEPS, c, x, off, gc[c]) for c in range(3)]
+                    m = m + tval[0, 2 * k, x] * (w[0] * g[0] + w[1] * g[1] + w[2] * g[2])
+                msum[x] = m
+                return carry
+
+            lax.fori_loop(0, bx, one, 0)
+
         def adjoint(n):
             gf = STEPS + n
-            roll_field(gf, rolled_g)
-            roll_field(n, rolled_u)
 
             def one(x, carry):
                 cent, shifted = centres(n, x)
@@ -353,15 +410,13 @@
                 m = jnp.zeros((8, nz), jnp.float32)
                 for k, rev, off in bond_list():
                     w = vectors(n, x, off, cent, shifted)
-                    g = [gc[c] - get(gf, rolled_g, c, x, off, gc[c]) for c in range(3)]
-                    n2 = float(sum(e * e for e in off))
-                    s = (w[0] * w[0] + w[1] * w[1] + w[2] * w[2]) - n2
+                    g = [gc[c] - get(gf, c, x, off, gc[c]) for c in range(3)]
                     dot = w[0] * g[0] + w[1] * g[1] + w[2] * g[2]
                     kk = coef(k, rev, x)
-                    t = kk * s
+                    t = kk * stretch(w, off) if n == STEPS - 1 else tval[n, 2 * k + rev, x]
                     r = kk * dot
-                    if not rev:
-                        m = m + s * r
+                    if n and not rev:
+                        m = m + t * dot
                     acc = [acc[c] + t * g[c] for c in range(3)]
                     bcc = [bcc[c] + r * w[c] for c in range(3)]
                 for c in range(3):
@@ -372,7 +427,8 @@
                     else:
                         out_a[c, x] = a
                         out_g[c, x] = gc[c]
-                msum[x] = m if n == STEPS - 1 else msum[x] + m
+                if n:
+                    msum[x] = m if n == STEPS - 1 else msum[x] + m
                 return carry
 
             lax.fori_loop(0, bx, one, 0)
@@ -380,13 +436,16 @@
         for n in range(STEPS - 1):
             forward(n)
             send_field(n + 1)
+            roll_own(n + 1)
+            if n == 0:
+                recv_field(2 * STEPS - 1)
             recv_field(n + 1)
-        recv_field(2 * STEPS - 1)
-        for n in reversed(range(STEPS)):
+        for n in range(STEPS - 1, 0, -1):
             adjoint(n)
-            if n:
-                send_field(STEPS + n - 1)
-                recv_field(STEPS + n - 1)
+            send_field(STEPS + n - 1)
+            roll_own(STEPS + n - 1)
+            recv_field(STEPS + n - 1)
+        micro_part()
 
         lane = lax.broadcasted_iota(jnp.int32, (1, nz), 1)
         row = jnp.zeros((1, nz), jnp.float32)
@@ -397,34 +456,35 @@
             one = jnp.sum(jnp.sum(tot, axis=0, keepdims=True), axis=1, keepdims=True)
             row = jnp.where(lane == cl, one * (TIME_STEP * inv_nodes) / micro[cl], row)
         mine[0] = row
-
-        def spread(src, land, axis_pos, size, ident, sems):
-            outs = []
-            for j in range(1, size):
-                cp = pltpu.make_async_remote_copy(
-                    src_ref=src, dst_ref=land.at[j - 1], send_sem=sems.at[0, j - 1], recv_sem=sems.at[1, j - 1],
-                    device_id=ident(lax.rem(axis_pos + j, size)), device_id_type=MESH,
-                )
-                cp.start()
-                outs.append(cp)
-            return outs
-
-        outs = spread(mine.at[0], part_x, ix, nx, lambda j: (j, iy), psem)
-        for cp in outs:
-            cp.wait_recv()
-        tot = mine[0]
-        for j in range(nx - 1):
-            tot = tot + part_x[j]
-        mine[1] = tot
-        outs_y = spread(mine.at[1], part_y, iy, ny, lambda j: (ix, j), qsem)
-        for cp in outs_y:
-            cp.wait_recv()
-        for j in range(ny - 1):
-            tot = tot + part_y[j]
+        part[me] = row
+
+        def share(j):
+            return pltpu.make_async_remote_copy(
+                src_ref=mine.at[0], dst_ref=part.at[me], send_sem=psem.at[j - 1], recv_sem=qsem.at[j - 1],
+                device_id=peer(j), device_id_type=MESH,
+            )
+
+        def give(j, carry):
+            share(j).start()
+            return carry
+
+        def take(j, carry):
+            share(j).wait_recv()
+            return carry
+
+        def gone(j, carry):
+            share(j).wait_send()
+            return carry
+
+        lax.fori_loop(1, nx * ny, give, 0)
+        adjoint(0)
+        lax.fori_loop(1, nx * ny, take, 0)
+        tot = part[0]
+        for j in range(1, nx * ny):
+            tot = tot + part[j]
         out_m[...] = tot
 
-        for cp in outs + outs_y:
-            cp.wait_send()
+        lax.fori_loop(1, nx * ny, gone, 0)
         for f in range(nf):
             for d in range(8):
                 @pl.when(there(*DIRS[d]))
@@ -447,6 +507,7 @@
         f32 = jnp.float32
         vmem = pl.BlockSpec(memory_space=pltpu.VMEM)
         smem = pl.BlockSpec(memory_space=pltpu.SMEM)
+        hbm = pl.BlockSpec(memory_space=pltpu.HBM)
         grad_a, grad_g, micro = pl.pallas_call(
             make_kernel(nx, ny, bx, by, nz),
             out_shape=(
@@ -454,12 +515,15 @@
                 jax.ShapeDtypeStruct((3, bx, by, nz), f32),
                 jax.ShapeDtypeStruct((1, nz), f32),
             ),
-            in_specs=[vmem] * 4 + [smem] + [vmem] * 2,
+            in_specs=[hbm] * 4 + [smem] + [hbm] * 2,
             out_specs=(vmem, vmem, vmem),
             scratch_shapes=[
                 pltpu.VMEM((nf, 3, bx + 4, 24, nz), f32),
-                pltpu.VMEM((2, 3, bx + 4, 24, nz), f32),
-                pltpu.VMEM((2, 3, bx + 4, 24, nz), f32),
+                pltpu.VMEM((nf, 2, 3, bx + 4, 24, nz), f32),
+                pltpu.VMEM((16, bx, 8, nz), jnp.int32),
+                pltpu.VMEM((bx, 8, nz), jnp.int32),
+                pltpu.VMEM((3, bx, 8, nz), f32),
+                pltpu.VMEM((STEPS - 1, 32, bx, 8, nz), f32),
                 pltpu.VMEM((16, bx + 4, 24, nz), f32),
                 pltpu.VMEM((16, bx, 8, nz), f32),
                 pltpu.VMEM((3, bx, 8, nz), f32),
@@ -467,6 +531,7 @@
                 pltpu.VMEM((bx, 8, nz), f32),
                 pltpu.VMEM((nf, 2, 6 * bx, nz), f32),
                 pltpu.VMEM((nf, 2, 6 * bx, nz), f32),
+                pltpu.VMEM((2, 6 * bx, nz), f32),
                 pltpu.VMEM((nf, 4, 16, nz), f32),
                 pltpu.VMEM((nf, 4, 16, nz), f32),
                 pltpu.VMEM((8 * bx, nz), f32),
@@ -475,15 +540,15 @@
                 pltpu.VMEM((3 * bx, nz), f32),
                 pltpu.VMEM((2, 8, nz), f32),
                 pltpu.VMEM((2, 8, nz), f32),
-                pltpu.VMEM((nx, 1, nz), f32),
-                pltpu.VMEM((ny, 1, nz), f32),
-                pltpu.VMEM((2, 1, nz), f32),
+                pltpu.VMEM((nx * ny, 1, nz), f32),
+                pltpu.VMEM((1, 1, nz), f32),
+                pltpu.SemaphoreType.DMA((6,)),
                 pltpu.SemaphoreType.DMA((nf, 8)),
                 pltpu.SemaphoreType.DMA((nf, 8)),
                 pltpu.SemaphoreType.DMA((6,)),
                 pltpu.SemaphoreType.DMA((6,)),
-                pltpu.SemaphoreType.DMA((2, nx)),
-                pltpu.SemaphoreType.DMA((2, ny)),
+                pltpu.SemaphoreType.DMA((nx * ny,)),
+                pltpu.SemaphoreType.DMA((nx * ny,)),
             ],
             compiler_params=pltpu.CompilerParams(
                 collective_id=0, has_side_effects=True, vmem_limit_bytes=40 * 1024 * 1024

time: 65.5 us -> 55.5 us (0.85)
  Pallas kernels: 56.7 us -> 46.7 us
    pallas_call x1, Pallas kernels: 56.7 us -> 46.7 us  [body(): pl.pallas_call(make_kernel(nx, ny, bx, by, nz), out_shape=(jax.ShapeDtype...]
where the time goes in v1:
time: 55.5 us; the launch traced here: 55.1 us
  Pallas kernels  46.7 us (84%)
  local copies, waits for them, and re-layouts  7.81 us (14%)
  between operations  0.66 us (1%)
    pallas_call x1, Pallas kernels, body(): pl.pallas_call(make_kernel(nx, ny, bx, by, nz), out_shape=(jax.ShapeDtype...  46.7 us
    unnamed x16, local copies, waits for them, and re-layouts  7.3 us

profile of v1, /device:TPU:0, one launch (start us, length us, event | category | flops | bytes accessed | tf_op | source)
XLA Modules:
  0.0 55.1 jit_solution(6592464424920922235)
XLA Ops:
  0.6 0.0 copy-start
  0.6 1.0 %copy-done = s32[16,8,8,128]{3,2,1,0:T(8,128)S(1)} copy-done((s32[16,8,8,128]{3,2,1,0:T(8,128)S(1)}, s32[16,8,8,128]{3,2,1,0:T(8,128)}, u32[]{:S(2)}) %copy-start) | copy-done | bytes 524312
  1.7 0.0 copy-start.1
  1.7 0.9 %copy-done.1 = f32[3,8,8,128]{3,2,1,0:T(8,128)S(1)} copy-done((f32[3,8,8,128]{3,2,1,0:T(8,128)S(1)}, f32[3,8,8,128]{3,2,1,0:T(8,128)}, u32[]{:S(2)}) %copy-start.1) | copy-done | bytes 98328
  2.6 0.0 copy-start.2
  2.6 0.9 %copy-done.2 = f32[3,8,8,128]{3,2,1,0:T(8,128)S(1)} copy-done((f32[3,8,8,128]{3,2,1,0:T(8,128)S(1)}, f32[3,8,8,128]{3,2,1,0:T(8,128)}, u32[]{:S(2)}) %copy-start.2) | copy-done | bytes 98328
  3.5 0.0 copy-start.3
  3.5 0.9 %copy-done.3 = f32[3,8,8,128]{3,2,1,0:T(8,128)S(1)} copy-done((f32[3,8,8,128]{3,2,1,0:T(8,128)S(1)}, f32[3,8,8,128]{3,2,1,0:T(8,128)}, u32[]{:S(2)}) %copy-start.3) | copy-done | bytes 98328
  4.4 0.0 copy-start.4
  4.4 0.9 %copy-done.4 = f32[3,8,8,128]{3,2,1,0:T(8,128)S(1)} copy-done((f32[3,8,8,128]{3,2,1,0:T(8,128)S(1)}, f32[3,8,8,128]{3,2,1,0:T(8,128)}, u32[]{:S(2)}) %copy-start.4) | copy-done | bytes 98328
  5.2 0.0 copy-start.5
  5.2 0.8 %copy-done.5 = s32[8,8,128]{2,1,0:T(8,128)S(1)} copy-done((s32[8,8,128]{2,1,0:T(8,128)S(1)}, s32[8,8,128]{2,1,0:T(8,128)}, u32[]{:S(2)}) %copy-start.5) | copy-done | bytes 32792
  6.0 0.0 copy-start.6
  6.0 0.7 %copy-done.6 = f32[8]{0:T(128)S(1)} copy-done((f32[8]{0:T(128)S(1)}, f32[8]{0:T(128)}, u32[]{:S(2)}) %copy-start.6) | copy-done | bytes 56
  6.7 46.7 %shard_map.94 = (f32[3,8,8,128]{3,2,1,0:T(8,128)S(1)}, f32[3,8,8,128]{3,2,1,0:T(8,128)S(1)}, f32[1,128]{1,0:T(1,128)S(1)}) custom-call(f32[3,8,8,128]{3,2,1,0:T(8,128)S(1)} %copy-done.1, f32[3,8,8,128]{3,2,1,0:T(8,128)S(1)} %copy-done.2, s32[16,8,8,128]{3,2,1,0:T(8,128)S(1)} %copy-done, s32[8,8,128]{2,1,0:T(8,128)S(1)} %copy-done.5, f32[8]{0:T(128)S(1)} %copy-done.6, ...), custom_call_target="tpu_custom_call" | custom-call | tf_op jit(solution)/shard_map/pallas_call | solution.py:511
  53.3 0.5 slice_bitcast_fusion
  53.8 0.6 %copy.12 = f32[3,8,8,128]{3,2,1,0:T(8,128)} copy(f32[3,8,8,128]{3,2,1,0:T(8,128)S(1)} %get-tuple-element.12) | data formatting | bytes 196608
  54.5 0.6 %copy.13 = f32[3,8,8,128]{3,2,1,0:T(8,128)} copy(f32[3,8,8,128]{3,2,1,0:T(8,128)S(1)} %get-tuple-element.13) | data formatting | bytes 196608
Async XLA Ops:
  0.6 1.0 %copy-start = (s32[16,8,8,128]{3,2,1,0:T(8,128)S(1)}, s32[16,8,8,128]{3,2,1,0:T(8,128)}, u32[]{:S(2)}) copy-start(s32[16,8,8,128]{3,2,1,0:T(8,128)} %cuts_in.1) | copy-start | bytes 1572868
  1.7 0.9 %copy-start.1 = (f32[3,8,8,128]{3,2,1,0:T(8,128)S(1)}, f32[3,8,8,128]{3,2,1,0:T(8,128)}, u32[]{:S(2)}) copy-start(f32[3,8,8,128]{3,2,1,0:T(8,128)} %disp.1) | copy-start | bytes 294916
  2.6 0.9 %copy-start.2 = (f32[3,8,8,128]{3,2,1,0:T(8,128)S(1)}, f32[3,8,8,128]{3,2,1,0:T(8,128)}, u32[]{:S(2)}) copy-start(f32[3,8,8,128]{3,2,1,0:T(8,128)} %vel.1) | copy-start | bytes 294916
  3.5 0.9 %copy-start.3 = (f32[3,8,8,128]{3,2,1,0:T(8,128)S(1)}, f32[3,8,8,128]{3,2,1,0:T(8,128)}, u32[]{:S(2)}) copy-start(f32[3,8,8,128]{3,2,1,0:T(8,128)} %cot_d.1) | copy-start | bytes 294916
  4.4 0.9 %copy-start.4 = (f32[3,8,8,128]{3,2,1,0:T(8,128)S(1)}, f32[3,8,8,128]{3,2,1,0:T(8,128)}, u32[]{:S(2)}) copy-start(f32[3,8,8,128]{3,2,1,0:T(8,128)} %cot_v.1) | copy-start | bytes 294916
  5.2 0.8 %copy-start.5 = (s32[8,8,128]{2,1,0:T(8,128)S(1)}, s32[8,8,128]{2,1,0:T(8,128)}, u32[]{:S(2)}) copy-start(s32[8,8,128]{2,1,0:T(8,128)} %material_in.1) | copy-start | bytes 98308
  6.0 0.7 %copy-start.6 = (f32[8]{0:T(128)S(1)}, f32[8]{0:T(128)}, u32[]{:S(2)}) copy-start(f32[8]{0:T(128)} %micro.1) | copy-start | bytes 100

commit v2 on v1

--- a/solution.py
+++ b/solution.py
@@ -56,7 +56,7 @@
 
 
 def make_kernel(nx, ny, bx, by, nz):
-    assert by == 8 and nz == 128
+    assert by == 8 and nz == 128 and bx % 4 == 0 and bx >= 8
     nf = 2 * STEPS
     inv_nodes = 1.0 / math.sqrt(nx * bx * ny * by * nz)
 
@@ -164,8 +164,8 @@
                 return carry
             lax.fori_loop(0, bx // 4, some, 0)
 
-        def recv_field(f):
-            for d in range(8):
+        def recv_field(f, dirs=range(8)):
+            for d in dirs:
                 sx, sy = DIRS[d]
                 y0 = Y0 - 2 if sy > 0 else Y0 + 8
                 near = Y0 - 1 if sy > 0 else Y0 + 8
@@ -366,7 +366,19 @@
         def stretch(w, off):
             return (w[0] * w[0] + w[1] * w[1] + w[2] * w[2]) - float(sum(e * e for e in off))
 
-        def forward(n):
+        ALONG_Y = (2, 3)
+        OTHERS = (0, 1, 4, 5, 6, 7)
+
+        def sweep(one, late):
+            def edge(i, carry):
+                return one(i + (i // 2) * (bx - 4), carry)
+
+            lax.fori_loop(2, bx - 2, one, 0)
+            if late is not None:
+                recv_field(late, OTHERS)
+            lax.fori_loop(0, 4, edge, 0)
+
+        def forward(n, late):
             def one(x, carry):
                 cent, shifted = centres(n, x)
                 acc = [jnp.zeros((8, nz), jnp.float32)] * 3
@@ -381,9 +393,9 @@
                     fld[n + 1, c, x + 2, pl.ds(Y0, 8), :] = cent[c] + TIME_STEP * v
                 return carry
 
-            lax.fori_loop(0, bx, one, 0)
-
-        def micro_part():
+            sweep(one, late)
+
+        def micro_part(late):
             def one(x, carry):
                 cent, shifted = centres(0, x)
                 gc = [fld[STEPS, c, x + 2, pl.ds(Y0, 8), :] for c in range(3)]
@@ -397,9 +409,9 @@
                 msum[x] = m
                 return carry
 
-            lax.fori_loop(0, bx, one, 0)
-
-        def adjoint(n):
+            sweep(one, late)
+
+        def adjoint(n, late):
             gf = STEPS + n
 
             def one(x, carry):
@@ -421,31 +433,30 @@
                     bcc = [bcc[c] + r * w[c] for c in range(3)]
                 for c in range(3):
                     a = anow[c, x] - TIME_STEP * (acc[c] + 2.0 * bcc[c])
+                    anow[c, x] = a
                     if n:
-                        anow[c, x] = a
                         fld[gf - 1, c, x + 2, pl.ds(Y0, 8), :] = gc[c] + TIME_STEP * a
-                    else:
-                        out_a[c, x] = a
-                        out_g[c, x] = gc[c]
                 if n:
                     msum[x] = m if n == STEPS - 1 else msum[x] + m
                 return carry
 
-            lax.fori_loop(0, bx, one, 0)
+            sweep(one, late)
 
         for n in range(STEPS - 1):
-            forward(n)
+            forward(n, n if n else None)
             send_field(n + 1)
             roll_own(n + 1)
             if n == 0:
                 recv_field(2 * STEPS - 1)
-            recv_field(n + 1)
+            recv_field(n + 1, ALONG_Y)
         for n in range(STEPS - 1, 0, -1):
-            adjoint(n)
+            adjoint(n, n if n == STEPS - 1 else STEPS + n)
             send_field(STEPS + n - 1)
             roll_own(STEPS + n - 1)
-            recv_field(STEPS + n - 1)
-        micro_part()
+            recv_field(STEPS + n - 1, ALONG_Y)
+        store_g = pltpu.make_async_copy(fld.at[STEPS, :, pl.ds(2, bx), pl.ds(Y0, 8), :], out_g, isem.at[0])
+        store_g.start()
+        micro_part(STEPS)
 
         lane = lax.broadcasted_iota(jnp.int32, (1, nz), 1)
         row = jnp.zeros((1, nz), jnp.float32)
@@ -477,12 +488,16 @@
             return carry
 
         lax.fori_loop(1, nx * ny, give, 0)
-        adjoint(0)
+        adjoint(0, None)
+        store_a = pltpu.make_async_copy(anow, out_a, isem.at[1])
+        store_a.start()
         lax.fori_loop(1, nx * ny, take, 0)
         tot = part[0]
         for j in range(1, nx * ny):
             tot = tot + part[j]
         out_m[...] = tot
+        store_g.wait()
+        store_a.wait()
 
         lax.fori_loop(1, nx * ny, gone, 0)
         for f in range(nf):
@@ -516,7 +531,7 @@
                 jax.ShapeDtypeStruct((1, nz), f32),
             ),
             in_specs=[hbm] * 4 + [smem] + [hbm] * 2,
-            out_specs=(vmem, vmem, vmem),
+            out_specs=(hbm, hbm, vmem),
             scratch_shapes=[
                 pltpu.VMEM((nf, 3, bx + 4, 24, nz), f32),
                 pltpu.VMEM((nf, 2, 3, bx + 4, 24, nz), f32),
@@ -551,7 +566,7 @@
                 pltpu.SemaphoreType.DMA((nx * ny,)),
             ],
             compiler_params=pltpu.CompilerParams(
-                collective_id=0, has_side_effects=True, vmem_limit_bytes=40 * 1024 * 1024
+                collective_id=0, has_side_effects=True, vmem_limit_bytes=63 * 1024 * 1024 + 768 * 1024
             ),
         )(displacement, velocity, cuts, material, micromodulus, cot_disp, cot_vel)
         return grad_a, grad_g, micro[0, :NCLASS]

time: 55.5 us -> 51.4 us (0.926)
  local copies, waits for them, and re-layouts: 7.81 us -> 3.36 us
    unnamed x16 -> x6, local copies, waits for them, and re-layouts: 7.3 us -> 2.85 us
where the time goes in v2:
time: 51.4 us; the launch traced here: 51.2 us
  Pallas kernels  47.2 us (92%)
  local copies, waits for them, and re-layouts  3.36 us (7%)
  between operations  0.65 us (1%)
    pallas_call x1, Pallas kernels, body(): pl.pallas_call(make_kernel(nx, ny, bx, by, nz), out_shape=(jax.ShapeDtype...  47.2 us
    unnamed x6, local copies, waits for them, and re-layouts  2.85 us

profile of v2, /device:TPU:0, one launch (start us, length us, event | category | flops | bytes accessed | tf_op | source)
XLA Modules:
  0.0 51.2 jit_solution(6646940789188712588)
XLA Ops:
  0.6 47.2 %shard_map.94 = (f32[3,8,8,128]{3,2,1,0:T(8,128)}, f32[3,8,8,128]{3,2,1,0:T(8,128)}, f32[1,128]{1,0:T(1,128)}) custom-call(f32[3,8,8,128]{3,2,1,0:T(8,128)} %disp.1, f32[3,8,8,128]{3,2,1,0:T(8,128)} %vel.1, s32[16,8,8,128]{3,2,1,0:T(8,128)} %cuts_in.1, s32[8,8,128]{2,1,0:T(8,128)} %material_in.1, f32[8]{0:T(128)} %micro.1, f32[3,8,8,128]{3,2,1,0:T(8,128)} %cot_d.1, ...), custom_call_target="tpu_custom_call" | custom-call | tf_op jit(solution)/shard_map/pallas_call | solution.py:526
  47.8 0.0 copy-start.1
  47.8 0.6 %copy-done.1 = f32[1,128]{1,0:T(1,128)S(1)} copy-done((f32[1,128]{1,0:T(1,128)S(1)}, f32[1,128]{1,0:T(1,128)}, u32[]{:S(2)}) %copy-start.1) | copy-done | bytes 536
  48.5 0.5 slice_bitcast_fusion
  49.0 0.0 copy-start
  49.0 1.6 %copy.12 = f32[3,8,8,128]{3,2,1,0:T(8,128)} copy(f32[3,8,8,128]{3,2,1,0:T(8,128)} %get-tuple-element.12) | data formatting | bytes 196608
  50.6 0.0 copy-done
  50.6 0.6 %copy.13 = f32[3,8,8,128]{3,2,1,0:T(8,128)} copy(f32[3,8,8,128]{3,2,1,0:T(8,128)S(1)} %copy-done) | data formatting | bytes 196608
Async XLA Ops:
  47.8 0.6 %copy-start.1 = (f32[1,128]{1,0:T(1,128)S(1)}, f32[1,128]{1,0:T(1,128)}, u32[]{:S(2)}) copy-start(f32[1,128]{1,0:T(1,128)} %get-tuple-element.8) | copy-start | bytes 1540
  49.0 1.6 %copy-start = (f32[3,8,8,128]{3,2,1,0:T(8,128)S(1)}, f32[3,8,8,128]{3,2,1,0:T(8,128)}, u32[]{:S(2)}) copy-start(f32[3,8,8,128]{3,2,1,0:T(8,128)} %get-tuple-element.13) | copy-start | bytes 294916
